TPU v7x, 32 devices: a whole 2x2x4 slice. The times are simulated.
32 devices in a mesh: groups: 2 (over x), ta: 16 (over z, y, core).
Axes of the slice: x: 2, y: 2, z: 4, core: 2. Of those that a mesh axis runs over, the one named last changes fastest.
Arguments:
- out_field: float32 [16, 64, 1024], P(None, ('groups', 'ta')), parts along dimension 1, may hold values from -6 to 6
- out_cot: float32 [16, 64, 1024], P(None, ('groups', 'ta')), parts along dimension 1, may hold values from -6 to 6
- jac_cot: float32 [64, 1024], P(('groups', 'ta')), parts along dimension 0, may hold values from -6 to 6
- mask: int32 [64, 1024], P(('groups', 'ta')), parts along dimension 0, may hold values 0 or 1
- perm: int32 [16], replicated, may hold values from 0 to 15, each once
- lower_param: float32 [16, 16], replicated, may hold values from -0.6 to 0.6
- upper_param: float32 [16, 16], replicated, may hold values from -0.6 to 0.6
- log_scale: float32 [16], replicated, may hold values from -0.3 to 0.3
- kern1: bfloat16 [81, 32, 16], replicated, may hold values from -0.15625 to 0.15625
- bias1: float32 [32], replicated, may hold values from -3 to 3
- kern2: bfloat16 [81, 32, 32], replicated, may hold values from -0.125 to 0.125
- bias2: float32 [32], replicated, may hold values from -2 to 2
Outputs:
- field_in: float32 [16, 64, 1024], P(None, ('groups', 'ta')), parts along dimension 1
- field_cot: float32 [16, 64, 1024], P(None, ('groups', 'ta')), parts along dimension 1
- grad_kern1: float32 [162, 32, 16], P('groups'), parts along dimension 0
- grad_bias1: float32 [64], P('groups'), parts along dimension 0
- grad_kern2: float32 [162, 32, 32], P('groups'), parts along dimension 0
- grad_bias2: float32 [64], P('groups'), parts along dimension 0
- grad_lower: float32 [32, 16], P('groups'), parts along dimension 0
- grad_upper: float32 [32, 16], P('groups'), parts along dimension 0
- grad_logs: float32 [32], P('groups'), parts along dimension 0
There are 2 independent parts, one for each index of `groups`. A program takes and returns all parts, laid end to end along the dimension named above; an argument that names none is the same for every part. Nothing has to cross between parts.
Inputs may be any that keep to these rules, and one draw needn't show every extreme that they name: `perm`: each of 0 to 15 exactly once.
All inputs are finite; a program needn't handle non-finite values. No bound on the sum of `mask` on one device may be relied on, other than what follows from the above.
Results may differ from a plain program's by a relative error of at most 0.0076.
Values may be sent and summed in bfloat16 or wider, within the bound.
A program may use at most 64 MiB of HBM per device.

v0:
```python
import functools
import math

import jax
import jax.numpy as jnp
from jax import lax
from jax.experimental import pallas as pl
from jax.experimental.pallas import tpu as pltpu
from jax.sharding import PartitionSpec as P

LX = 8
LY = 8
LZ = 16
ROW = LY * LZ

HIGH = lax.Precision.HIGHEST
F32 = jnp.float32
BF16 = jnp.bfloat16
VMEM_LIMIT = 48 * 1024 * 1024


def dot(a, b, precision=None):
    return lax.dot_general(
        a, b, (((1,), (0,)), ((), ())), precision=precision, preferred_element_type=F32
    )


def dot_tn(a, b, precision=None):
    return lax.dot_general(
        a, b, (((0,), (0,)), ((), ())), precision=precision, preferred_element_type=F32
    )


def dot_nt(a, b, precision=None):
    return lax.dot_general(
        a, b, (((1,), (1,)), ((), ())), precision=precision, preferred_element_type=F32
    )


def iota(shape, dim):
    return lax.broadcasted_iota(jnp.int32, shape, dim)


def column(row):
    count = row.shape[1]
    same = iota((count, count), 0) == iota((count, count), 1)
    return jnp.sum(jnp.where(same, row, 0.0), axis=1, keepdims=True)


def nilpotent_inverse(nilpart):
    count = nilpart.shape[0]
    eye = jnp.where(iota((count, count), 0) == iota((count, count), 1), 1.0, 0.0)
    result = eye - nilpart
    power = dot(nilpart, nilpart, HIGH)
    span = 2
    while span < count:
        result = dot(result, eye + power, HIGH)
        power = dot(power, power, HIGH)
        span = span * 2
    return result


def factors(perm_row, lower_param, upper_param, log_row):
    chans = lower_param.shape[0]
    rows, cols = iota((chans, chans), 0), iota((chans, chans), 1)
    strict_low = jnp.where(rows > cols, lower_param, 0.0)
    strict_up = jnp.where(cols > rows, upper_param, 0.0)
    diag = column(jnp.exp(log_row))
    perm_t = jnp.where(rows == perm_row, 1.0, 0.0)
    lower_tri = strict_low + jnp.where(rows == cols, 1.0, 0.0)
    upper_tri = strict_up + jnp.where(rows == cols, diag, 0.0)
    return strict_low, strict_up, lower_tri, upper_tri, perm_t, diag


def to_tiles(v):
    return jnp.concatenate([v[:, x * ROW : (x + 1) * ROW] for x in range(LX)], axis=0)


def to_lanes(v):
    chans = v.shape[0] // LX
    return jnp.concatenate([v[x * chans : (x + 1) * chans] for x in range(LX)], axis=1)


def shift_z(v, off):
    if off == 0:
        return v
    z = iota(v.shape, 1) % LZ
    if off > 0:
        return jnp.where(z == LZ - 1, pltpu.roll(v, LZ - 1, 1), pltpu.roll(v, ROW - 1, 1))
    return jnp.where(z == 0, pltpu.roll(v, ROW - LZ + 1, 1), pltpu.roll(v, 1, 1))


def shift_y(v, off):
    if off == 0:
        return v
    return pltpu.roll(v, (ROW - off * LZ) % ROW, 1)


def shift_x(v, off):
    if off == 0:
        return v
    if off > 0:
        return jnp.concatenate([v[:, ROW:], v[:, :ROW]], axis=1)
    return jnp.concatenate([v[:, -ROW:], v[:, :-ROW]], axis=1)


def store_plane_stack(ref, slot, v):
    chans = v.shape[0]
    tiles = to_tiles(v)
    along_z = [shift_z(tiles, e) for e in (-1, 0, 1)]
    for c in (-1, 0, 1):
        for e in (-1, 0, 1):
            k = 3 * (c + 1) + e + 1
            piece = to_lanes(shift_y(along_z[e + 1], c)).astype(BF16)
            ref[slot, k * chans : (k + 1) * chans, :] = piece


def unstack_plane(q):
    chans = q.shape[0] // 9
    total = None
    for e in (-1, 0, 1):
        along = None
        for c in (-1, 0, 1):
            k = 3 * (c + 1) + e + 1
            piece = shift_y(to_tiles(q[k * chans : (k + 1) * chans]), -c)
            along = piece if along is None else along + piece
        along = shift_z(along, -e)
        total = along if total is None else total + along
    return to_lanes(total)


def valid_taps(source, count):
    taps = [a for a in (-1, 0, 1) if 0 <= source - a < count]
    return taps[0], taps[-1] + 1


def add_forward(outs, weight, stack, source):
    first, end = valid_taps(source, len(outs))
    hid = weight.shape[0] // 9
    prod = dot(weight[3 * hid * (first + 1) : 3 * hid * (end + 1), :], stack)
    for a in range(first, end):
        for b in (-1, 0, 1):
            lo = (3 * (a - first) + b + 1) * hid
            piece = shift_x(prod[lo : lo + hid], b)
            t = source - a
            outs[t] = piece if outs[t] is None else outs[t] + piece


def spread_stack(slices, taps):
    return jnp.concatenate(
        [shift_x(slices[i], -b) for i in range(len(taps)) for b in (-1, 0, 1)], axis=0
    )


def kernel_grads(cot, stacks, count):
    blocks = {}
    for source in range(-1, count + 1):
        first, end = valid_taps(source, count)
        taps = list(range(first, end))
        left = spread_stack([cot[source - a] for a in taps], taps)
        prod = dot_nt(left, stacks(source))
        for i, a in enumerate(taps):
            size = left.shape[0] // len(taps)
            part = prod[i * size : (i + 1) * size]
            blocks[a] = part if a not in blocks else blocks[a] + part
    return jnp.concatenate([blocks[a] for a in (-1, 0, 1)], axis=0)


def to_blocks(grad, fold):
    rows, cols = grad.shape
    full = cols // 128
    rest = cols - full * 128
    parts = [grad[:, i * 128 : (i + 1) * 128] for i in range(full)]
    tail = grad[:, full * 128 :]
    each = rows // fold
    tails = [tail[i * each : (i + 1) * each] for i in range(fold)]
    tails.append(jnp.zeros((each, 128 - rest * fold), F32))
    parts.append(jnp.concatenate(tails, axis=1))
    return jnp.concatenate(parts, axis=0)


def from_blocks(packed, rows, cols, fold):
    full = cols // 128
    rest = cols - full * 128
    each = rows // fold
    parts = [packed[i * rows : (i + 1) * rows] for i in range(full)]
    last = packed[full * rows : full * rows + each]
    tail = jnp.concatenate([last[:, i * rest : (i + 1) * rest] for i in range(fold)], axis=0)
    return jnp.concatenate(parts + [tail], axis=1)


def block_rows(rows, cols, fold, n):
    total = (cols // 128) * rows + rows // fold
    blocks = -(-total // 16)
    return total, 16 * -(-blocks // n)


FOLD1 = 3
FOLD2 = 1


def main_kernel(
    n,
    out_field,
    out_cot,
    jac,
    mask,
    perm,
    lower,
    upper,
    logs,
    kern1,
    bias1,
    kern2,
    bias2,
    field_in_o,
    field_cot_o,
    gath1_o,
    gath2_o,
    small_o,
    frozen,
    stack1,
    stack2,
    ncot,
    pcot,
    w1,
    w1t,
    w2,
    w2t,
    send1,
    recv1,
    gath1,
    send2,
    recv2,
    gath2,
    small_mine,
    small_all,
    halo_send,
    halo_recv,
    s1_send,
    s1_recv,
    s2_send,
    s2_recv,
    g1_send,
    g1_recv,
    g2_send,
    g2_recv,
    sm_send,
    sm_recv,
):
    me = lax.axis_index("ta")
    chans, count, sites = out_field.shape
    hid = kern1.shape[2]
    right, left = lax.rem(me + 1, n), lax.rem(me + n - 1, n)

    barrier = pltpu.get_barrier_semaphore()

    def greet(k, carry):
        pl.semaphore_signal(barrier, inc=1, device_id={"ta": lax.rem(me + k, n)})
        return carry

    lax.fori_loop(1, n, greet, 0)

    strict_low, strict_up, lower_tri, upper_tri, perm_t, diag = factors(
        perm[...], lower[...], upper[...], logs[...]
    )
    inv_diag_row = jnp.exp(logs[...])
    upper_inv = nilpotent_inverse(strict_up / diag) * (1.0 / inv_diag_row)
    lower_inv = nilpotent_inverse(strict_low)
    unmixer = dot(dot(upper_inv, lower_inv, HIGH), perm_t, HIGH)
    mixer = dot_tn(perm_t, dot(lower_tri, upper_tri, HIGH), HIGH)

    keep = [mask[t : t + 1, :].astype(F32) for t in range(count)]
    coupled = [dot(unmixer, out_field[:, t, :], HIGH) for t in range(count)]
    for t in range(count):
        frozen[2 + t] = (keep[t] * coupled[t]).astype(BF16)

    pl.semaphore_wait(barrier, n - 1)

    def halo(index, src, dst, where):
        return pltpu.make_async_remote_copy(
            src_ref=src,
            dst_ref=dst,
            send_sem=halo_send.at[index],
            recv_sem=halo_recv.at[index],
            device_id={"ta": where},
        )

    def exchange(base, buf, width):
        up = halo(base, buf.at[pl.ds(count, width)], buf.at[pl.ds(0, width)], right)
        down = halo(
            base + 1, buf.at[pl.ds(width, width)], buf.at[pl.ds(width + count, width)], left
        )
        up.start()
        down.start()
        return up, down

    first_halo = exchange(0, frozen, 2)

    def spread(send, recv, s_sem, r_sem):
        def step(k, carry):
            peer = lax.rem(me + k, n)
            pltpu.make_async_remote_copy(
                src_ref=send.at[peer],
                dst_ref=recv.at[k],
                send_sem=s_sem.at[k],
                recv_sem=r_sem.at[k],
                device_id={"ta": peer},
            ).start()
            return carry

        lax.fori_loop(1, n, step, 0)

    def collect(send, recv, s_sem, r_sem):
        def step(k, total):
            peer = lax.rem(me + k, n)
            pltpu.make_async_remote_copy(
                src_ref=send.at[peer],
                dst_ref=recv.at[k],
                send_sem=s_sem.at[k],
                recv_sem=r_sem.at[k],
                device_id={"ta": peer},
            ).wait()
            return total + recv[k].astype(F32)

        return lax.fori_loop(1, n, step, send[me].astype(F32))

    def share(buf, s_sem, r_sem):
        def step(k, carry):
            pltpu.make_async_remote_copy(
                src_ref=buf.at[me],
                dst_ref=buf.at[me],
                send_sem=s_sem.at[k],
                recv_sem=r_sem.at[k],
                device_id={"ta": lax.rem(me + k, n)},
            ).start()
            return carry

        lax.fori_loop(1, n, step, 0)

    def share_done(buf, s_sem, r_sem):
        def step(k, carry):
            peer = lax.rem(me + n - k, n)
            done = pltpu.make_async_remote_copy(
                src_ref=buf.at[me],
                dst_ref=buf.at[peer],
                send_sem=s_sem.at[k],
                recv_sem=r_sem.at[k],
                device_id={"ta": lax.rem(me + k, n)},
            )
            done.wait_recv()
            done.wait_send()
            return carry

        lax.fori_loop(1, n, step, 0)

    for kern, w, wt in ((kern1, w1, w1t), (kern2, w2, w2t)):
        ins = kern.shape[3]
        wide = jnp.concatenate(
            [kern[:, k].astype(F32).reshape(9 * hid, ins) for k in range(9)], axis=1
        )
        w[...] = wide.astype(BF16)
        wt[...] = wide.T.astype(BF16)

    coupled_cot = [dot_tn(mixer, out_cot[:, t, :], HIGH) for t in range(count)]
    mix = None
    for t in range(count):
        term = dot_nt(out_cot[:, t, :], coupled[t], HIGH)
        mix = term if mix is None else mix + term
    jac_sum = jnp.sum(jnp.sum(jac[...], axis=1, keepdims=True), axis=0, keepdims=True)

    hidden_pre = [None] * (count + 2)
    for slot in range(2, count + 2):
        store_plane_stack(stack1, slot, frozen[slot].astype(F32))
        add_forward(hidden_pre, w1, stack1[slot], slot - 1)
    for copy in first_halo:
        copy.wait()
    for slot in [0, 1] + [count + 2, count + 3]:
        store_plane_stack(stack1, slot, frozen[slot].astype(F32))
        add_forward(hidden_pre, w1, stack1[slot], slot - 1)

    bias1_col = column(bias1[...])
    bias2_col = column(bias2[...])
    net = [None] * count
    hidden_mid = []
    for slot in range(count + 2):
        hidden = jnp.tanh(hidden_pre[slot] + bias1_col).astype(BF16).astype(F32)
        if 1 <= slot <= count:
            hidden_mid.append(hidden)
        store_plane_stack(stack2, slot, hidden)
        add_forward(net, w2, stack2[slot], slot - 1)

    growth = []
    cots = []
    for t in range(count):
        net_t = net[t] + bias2_col
        scale = jnp.tanh(net_t[:chans])
        shift = net_t[chans:]
        free = 1.0 - keep[t]
        grow = jnp.exp(scale)
        growth.append(grow)
        fin = keep[t] * coupled[t] + free * (coupled[t] - shift) * jnp.exp(-scale)
        field_in_o[:, t, :] = fin
        scale_cot = free * (coupled_cot[t] * fin * grow + jac[t : t + 1, :])
        cot = jnp.concatenate(
            [scale_cot * (1.0 - scale * scale), free * coupled_cot[t]], axis=0
        ).astype(BF16)
        ncot[1 + t] = cot
        cots.append(cot)
    second_halo = exchange(2, ncot, 1)

    grads2 = kernel_grads(cots, lambda s: stack2[s + 1], count)
    total2, rows2 = block_rows(9 * hid, 9 * hid, FOLD2, n)
    packed2 = to_blocks(grads2, FOLD2)
    packed2 = jnp.concatenate(
        [packed2, jnp.zeros((n * rows2 - total2, 128), F32)], axis=0
    ).astype(BF16)
    for p in range(n):
        send2[p] = packed2[p * rows2 : (p + 1) * rows2]
    spread(send2, recv2, s2_send, s2_recv)

    ones = jnp.ones((8, sites), BF16)
    bias2_row = sum(dot_nt(ones, c) for c in cots)

    for copy in second_halo:
        copy.wait()
    pres = []
    for t in range(count):
        taps = (-1, 0, 1)
        wide = spread_stack([ncot[1 + t - a] for a in taps], taps)
        hidden_cot = unstack_plane(dot(w2t[...], wide))
        pre = (hidden_cot * (1.0 - hidden_mid[t] * hidden_mid[t])).astype(BF16)
        pcot[1 + t] = pre
        pres.append(pre)
    third_halo = exchange(4, pcot, 1)

    grads1 = kernel_grads(pres, lambda s: stack1[s + 2], count)
    total1, rows1 = block_rows(9 * hid, 9 * chans, FOLD1, n)
    packed1 = to_blocks(grads1, FOLD1)
    packed1 = jnp.concatenate(
        [packed1, jnp.zeros((n * rows1 - total1, 128), F32)], axis=0
    ).astype(BF16)
    for p in range(n):
        send1[p] = packed1[p * rows1 : (p + 1) * rows1]
    spread(send1, recv1, s1_send, s1_recv)

    bias1_row = sum(dot_nt(ones, c) for c in pres)
    small_mine[...] = jnp.concatenate(
        [mix[:8], mix[8:], bias1_row, bias2_row, jnp.broadcast_to(jac_sum, (8, 32))], axis=1
    )

    def small_copy(k):
        return pltpu.make_async_remote_copy(
            src_ref=small_mine,
            dst_ref=small_all.at[k],
            send_sem=sm_send.at[k],
            recv_sem=sm_recv.at[k],
            device_id={"ta": lax.rem(me + k, n)},
        )

    def small_start(k, carry):
        small_copy(k).start()
        return carry

    lax.fori_loop(1, n, small_start, 0)

    gath2[me] = collect(send2, recv2, s2_send, s2_recv).astype(BF16)
    share(gath2, g2_send, g2_recv)

    for copy in third_halo:
        copy.wait()
    for t in range(count):
        taps = (-1, 0, 1)
        wide = spread_stack([pcot[1 + t - a] for a in taps], taps)
        frozen_cot = unstack_plane(dot(w1t[...], wide))
        free = 1.0 - keep[t]
        field_cot_o[:, t, :] = (
            keep[t] * (coupled_cot[t] + frozen_cot) + free * coupled_cot[t] * growth[t]
        )

    gath1[me] = collect(send1, recv1, s1_send, s1_recv).astype(BF16)
    share(gath1, g1_send, g1_recv)

    def small_done(k, carry):
        small_copy(k).wait()
        return carry

    lax.fori_loop(1, n, small_done, 0)
    small_all[0] = small_mine[...]

    def small_add(k, total):
        return total + small_all[lax.rem(me + n - k, n)]

    small_o[...] = lax.fori_loop(0, n, small_add, jnp.zeros(small_mine.shape, F32))

    share_done(gath2, g2_send, g2_recv)
    gath2_o[...] = gath2[...]
    share_done(gath1, g1_send, g1_recv)
    gath1_o[...] = gath1[...]


def last_kernel(
    norm,
    field_in,
    field_cot,
    gath1,
    gath2,
    small,
    perm,
    lower,
    upper,
    logs,
    field_in_o,
    field_cot_o,
    kern1_o,
    bias1_o,
    kern2_o,
    bias2_o,
    lower_o,
    upper_o,
    logs_o,
):
    field_in_o[...] = field_in[...]
    field_cot_o[...] = field_cot[...]
    for gath, out, fold in ((gath1, kern1_o, FOLD1), (gath2, kern2_o, FOLD2)):
        hid, ins = out.shape[2], out.shape[3]
        grid = from_blocks(gath[...].astype(F32) * norm, 9 * hid, 9 * ins, fold)
        for k in range(9):
            out[:, k] = grid[:, k * ins : (k + 1) * ins].reshape(9, hid, ins)
    _, _, lower_tri, upper_tri, perm_t, _ = factors(
        perm[...], lower[...], upper[...], logs[...]
    )
    sums = small[...] * norm
    chans = lower.shape[0]
    hid = bias1_o.shape[1]
    mix = jnp.concatenate([sums[:, :chans], sums[:, chans : 2 * chans]], axis=0)
    base = 2 * chans
    bias1_o[...] = sums[0:1, base : base + hid]
    bias2_o[...] = sums[0:1, base + hid : base + 2 * hid]
    turned = dot(perm_t, mix, HIGH)
    lower_full = dot_nt(turned, upper_tri, HIGH)
    upper_full = dot_tn(lower_tri, turned, HIGH)
    rows, cols = iota((chans, chans), 0), iota((chans, chans), 1)
    lower_o[...] = jnp.where(rows > cols, lower_full, 0.0)
    upper_o[...] = jnp.where(cols > rows, upper_full, 0.0)
    diag = jnp.sum(jnp.where(rows == cols, upper_full, 0.0), axis=0, keepdims=True)
    jac_row = sums[0:1, base + 2 * hid : base + 2 * hid + chans]
    logs_o[...] = diag * jnp.exp(logs[...]) + jac_row


def body(
    n,
    out_field,
    out_cot,
    jac_cot,
    mask,
    perm,
    lower_param,
    upper_param,
    log_scale,
    kern1,
    bias1,
    kern2,
    bias2,
):
    chans, count, sites = out_field.shape
    hid = kern1.shape[1]
    perm_row = perm.reshape(1, chans)
    log_row = log_scale.reshape(1, chans)
    _, rows1 = block_rows(9 * hid, 9 * chans, FOLD1, n)
    _, rows2 = block_rows(9 * hid, 9 * hid, FOLD2, n)
    vmem = pl.BlockSpec(memory_space=pltpu.VMEM)
    shape = jax.ShapeDtypeStruct
    field = shape((chans, count, sites), F32)
    dma = pltpu.SemaphoreType.DMA
    field_in, field_cot, gath1, gath2, small = pl.pallas_call(
        functools.partial(main_kernel, n),
        out_shape=(
            field,
            field,
            shape((n, rows1, 128), BF16),
            shape((n, rows2, 128), BF16),
            shape((8, 128), F32),
        ),
        in_specs=[vmem] * 12,
        out_specs=(vmem,) * 5,
        scratch_shapes=[
            pltpu.VMEM((count + 4, chans, sites), BF16),
            pltpu.VMEM((count + 4, 9 * chans, sites), BF16),
            pltpu.VMEM((count + 2, 9 * hid, sites), BF16),
            pltpu.VMEM((count + 2, hid, sites), BF16),
            pltpu.VMEM((count + 2, hid, sites), BF16),
            pltpu.VMEM((9 * hid, 9 * chans), BF16),
            pltpu.VMEM((9 * chans, 9 * hid), BF16),
            pltpu.VMEM((9 * hid, 9 * hid), BF16),
            pltpu.VMEM((9 * hid, 9 * hid), BF16),
        ]
        + [pltpu.VMEM((n, rows1, 128), BF16)] * 3
        + [pltpu.VMEM((n, rows2, 128), BF16)] * 3
        + [pltpu.VMEM((8, 128), F32), pltpu.VMEM((n, 8, 128), F32)]
        + [dma((6,))] * 2
        + [dma((n,))] * 10,
        compiler_params=pltpu.CompilerParams(
            collective_id=0, has_side_effects=True, vmem_limit_bytes=VMEM_LIMIT
        ),
        name="block_backward",
    )(
        out_field,
        out_cot,
        jac_cot,
        mask,
        perm_row,
        lower_param,
        upper_param,
        log_row,
        kern1.reshape(9, 9, hid, chans),
        bias1.reshape(1, hid),
        kern2.reshape(9, 9, kern2.shape[1], hid),
        bias2.reshape(1, -1),
    )
    norm = 1.0 / math.sqrt(count * sites * n)
    outs = pl.pallas_call(
        functools.partial(last_kernel, norm),
        out_shape=(
            field,
            field,
            shape((9, 9, hid, chans), F32),
            shape((1, hid), F32),
            shape((9, 9, 2 * chans, hid), F32),
            shape((1, 2 * chans), F32),
            shape((chans, chans), F32),
            shape((chans, chans), F32),
            shape((1, chans), F32),
        ),
        in_specs=[vmem] * 9,
        out_specs=(vmem,) * 9,
        compiler_params=pltpu.CompilerParams(vmem_limit_bytes=VMEM_LIMIT),
        name="unpack",
    )(
        field_in,
        field_cot,
        gath1.reshape(n * rows1, 128),
        gath2.reshape(n * rows2, 128),
        small,
        perm_row,
        lower_param,
        upper_param,
        log_row,
    )
    return (
        outs[0],
        outs[1],
        outs[2].reshape(81, hid, chans),
        outs[3].reshape(-1),
        outs[4].reshape(81, 2 * chans, hid),
        outs[5].reshape(-1),
        outs[6],
        outs[7],
        outs[8].reshape(-1),
    )


def solution(mesh):
    split = ("groups", "ta")
    in_specs = (
        P(None, split, None),
        P(None, split, None),
        P(split, None),
        P(split, None),
    ) + (P(),) * 8
    out_specs = (
        P(None, split, None),
        P(None, split, None),
        P("groups", None, None),
        P("groups"),
        P("groups", None, None),
        P("groups"),
        P("groups", None),
        P("groups", None),
        P("groups"),
    )
    return jax.shard_map(
        functools.partial(body, mesh.shape["ta"]),
        mesh=mesh,
        in_specs=in_specs,
        out_specs=out_specs,
        check_vma=False,
    )
```

profile of v0, /device:TPU:0, one launch (start us, length us, event | category | flops | bytes accessed | tf_op | source)
XLA Modules:
  0.0 45.6 jit_solution(6712937431938807207)
XLA Ops:
  0.6 0.0 copy-start.3
  0.7 0.0 copy-start.2
  0.7 0.0 copy-start.9
  0.7 0.0 copy-start.8
  0.7 0.0 copy-start.7
  0.7 0.0 copy-start.6
  0.7 0.0 copy-start.5
  0.7 0.0 copy-start.4
  0.7 0.0 copy-start.1
  0.7 0.0 copy-start
  0.7 2.0 %copy.21 = bf16[81,32,16]{2,1,0:T(8,128)(2,1)S(1)} copy(bf16[81,32,16]{0,2,1:T(8,128)(2,1)} %param.20) | data formatting | bytes 165888 | tf_op args[8]
  2.8 2.0 %copy.22 = bf16[81,32,32]{2,1,0:T(8,128)(2,1)S(1)} copy(bf16[81,32,32]{0,2,1:T(8,128)(2,1)} %param.22) | data formatting | bytes 331776 | tf_op args[10]
  4.8 0.0 copy-done.3
  4.8 0.0 copy-done.2
  4.8 0.0 copy-done.9
  4.8 0.0 copy-done.8
  4.8 0.0 copy-done.7
  4.8 0.0 copy-done.6
  4.9 0.0 copy-done.5
  4.9 0.0 copy-done.4
  4.9 0.0 copy-done.1
  4.9 0.0 copy-done
  4.9 36.2 %block_backward.1 = (f32[16,2,1024]{2,1,0:T(2,128)S(1)}, f32[16,2,1024]{2,1,0:T(2,128)S(1)}, bf16[16,32,128]{2,1,0:T(8,128)(2,1)S(1)}, bf16[16,64,128]{2,1,0:T(8,128)(2,1)S(1)}, f32[8,128]{1,0:T(8,128)S(1)}) custom-call(f32[16,2,1024]{2,1,0:T(2,128)S(1)} %copy-done, f32[16,2,1024]{2,1,0:T(2,128)S(1)} %copy-done.1, f32[2,1024]{1,0:T(2,128)S(1)} %copy-done.4, ...), custom_call_target="tpu_custom_call" | custom-call | tf_op jit(solution)/shard_map/block_backward/pallas_call | solution.py:576
  41.1 1.3 %unpack.1 = (f32[16,2,1024]{2,1,0:T(2,128)}, f32[16,2,1024]{2,1,0:T(2,128)}, f32[9,9,32,16]{3,2,1,0:T(8,128)S(1)}, f32[1,32]{1,0:T(1,128)}, f32[9,9,32,32]{3,2,1...) custom-call(f32[16,2,1024]{2,1,0:T(2,128)S(1)} %get-tuple-element.23.field_in, ...), custom_call_target="tpu_custom_call" | custom-call | tf_op jit(solution)/shard_map/unpack/pallas_call | solution.py:622
  42.4 1.6 %copy.23 = f32[81,32,16]{0,2,1:T(8,128)} copy(f32[81,32,16]{2,1,0:T(8,128)S(1)} %bitcast.16) | data formatting | bytes 331776
  43.9 1.7 %copy.24 = f32[81,32,32]{0,2,1:T(8,128)} copy(f32[81,32,32]{2,1,0:T(8,128)S(1)} %bitcast.15) | data formatting | bytes 663552
Async XLA Ops:
  0.6 4.2 %copy-start.3 = (f32[16,16]{1,0:T(8,128)S(1)}, f32[16,16]{1,0:T(8,128)}, u32[]{:S(2)}) copy-start(f32[16,16]{1,0:T(8,128)} %upper.3) | copy-start | bytes 3076
  0.7 4.2 %copy-start.2 = (f32[16,16]{1,0:T(8,128)S(1)}, f32[16,16]{1,0:T(8,128)}, u32[]{:S(2)}) copy-start(f32[16,16]{1,0:T(8,128)} %lower.3) | copy-start | bytes 3076
  0.7 4.2 %copy-start.9 = (f32[32]{0:T(128)S(1)}, f32[32]{0:T(128)}, u32[]{:S(2)}) copy-start(f32[32]{0:T(128)} %param.23) | copy-start | bytes 388
  0.7 4.2 %copy-start.8 = (f32[32]{0:T(128)S(1)}, f32[32]{0:T(128)}, u32[]{:S(2)}) copy-start(f32[32]{0:T(128)} %param.21) | copy-start | bytes 388
  0.7 4.2 %copy-start.7 = (f32[16]{0:T(128)S(1)}, f32[16]{0:T(128)}, u32[]{:S(2)}) copy-start(f32[16]{0:T(128)} %param.19) | copy-start | bytes 196
  0.7 4.2 %copy-start.6 = (s32[16]{0:T(128)S(1)}, s32[16]{0:T(128)}, u32[]{:S(2)}) copy-start(s32[16]{0:T(128)} %param.16) | copy-start | bytes 196
  0.7 4.2 %copy-start.5 = (s32[2,1024]{1,0:T(2,128)S(1)}, s32[2,1024]{1,0:T(2,128)}, u32[]{:S(2)}) copy-start(s32[2,1024]{1,0:T(2,128)} %mask.1) | copy-start | bytes 24580
  0.7 4.2 %copy-start.4 = (f32[2,1024]{1,0:T(2,128)S(1)}, f32[2,1024]{1,0:T(2,128)}, u32[]{:S(2)}) copy-start(f32[2,1024]{1,0:T(2,128)} %jac.1) | copy-start | bytes 24580
  0.7 4.2 %copy-start.1 = (f32[16,2,1024]{2,1,0:T(2,128)S(1)}, f32[16,2,1024]{2,1,0:T(2,128)}, u32[]{:S(2)}) copy-start(f32[16,2,1024]{2,1,0:T(2,128)} %out_cot.1) | copy-start | bytes 393220
  0.7 4.2 %copy-start = (f32[16,2,1024]{2,1,0:T(2,128)S(1)}, f32[16,2,1024]{2,1,0:T(2,128)}, u32[]{:S(2)}) copy-start(f32[16,2,1024]{2,1,0:T(2,128)} %out_field.1) | copy-start | bytes 393220
where the time goes:
time: 45.8 us; the launch traced here: 45.6 us
  Pallas kernels  37.5 us (82%)
  local copies, waits for them, and re-layouts  7.34 us (16%)
  between operations  0.81 us (2%)
    pallas_call x1, Pallas kernels, body(): pl.pallas_call(functools.partial(main_kernel, n), out_shape=(field, field...  36.2 us
    unnamed x24, local copies, waits for them, and re-layouts  7.34 us
    pallas_call x1, Pallas kernels, body(): pl.pallas_call(functools.partial(last_kernel, norm), out_shape=(field, fi...  1.3 us

commit v1 on v0

--- a/solution.py
+++ b/solution.py
@@ -35,6 +35,20 @@
     return lax.dot_general(
         a, b, (((1,), (1,)), ((), ())), precision=precision, preferred_element_type=F32
     )
+
+
+def split3(v):
+    first = v.astype(BF16)
+    rest = v - first.astype(F32)
+    second = rest.astype(BF16)
+    return first, second, (rest - second.astype(F32)).astype(BF16)
+
+
+def mix_field(matrix, pieces):
+    m1, m2, m3 = (m.astype(F32) for m in split3(matrix))
+    x1, x2, x3 = pieces
+    left = jnp.concatenate([m1, m1, m1, m2, m2, m3], axis=1).astype(BF16)
+    return dot(left, jnp.concatenate([x1, x2, x3, x1, x2, x1], axis=0))
 
 
 def iota(shape, dim):
@@ -228,13 +242,19 @@
     w2,
     w2t,
     send1,
+    gath1,
+    paired1,
     recv1,
-    gath1,
     send2,
+    gath2,
+    paired2,
     recv2,
-    gath2,
     small_mine,
+    small_other,
     small_all,
+    p1_sem,
+    p2_sem,
+    ps_sem,
     halo_send,
     halo_recv,
     s1_send,
@@ -247,11 +267,19 @@
     g2_recv,
     sm_send,
     sm_recv,
+    f1_send,
+    f1_recv,
+    f2_send,
+    f2_recv,
 ):
     me = lax.axis_index("ta")
     chans, count, sites = out_field.shape
     hid = kern1.shape[2]
     right, left = lax.rem(me + 1, n), lax.rem(me + n - 1, n)
+    chips = n // 2
+    chip, core = me // 2, lax.rem(me, 2)
+    other = 1 - core
+    partner = 2 * chip + other
 
     barrier = pltpu.get_barrier_semaphore()
 
@@ -268,10 +296,10 @@
     upper_inv = nilpotent_inverse(strict_up / diag) * (1.0 / inv_diag_row)
     lower_inv = nilpotent_inverse(strict_low)
     unmixer = dot(dot(upper_inv, lower_inv, HIGH), perm_t, HIGH)
-    mixer = dot_tn(perm_t, dot(lower_tri, upper_tri, HIGH), HIGH)
+    mixer_t = dot_tn(dot(lower_tri, upper_tri, HIGH), perm_t, HIGH)
 
     keep = [mask[t : t + 1, :].astype(F32) for t in range(count)]
-    coupled = [dot(unmixer, out_field[:, t, :], HIGH) for t in range(count)]
+    coupled = [mix_field(unmixer, split3(out_field[:, t, :])) for t in range(count)]
     for t in range(count):
         frozen[2 + t] = (keep[t] * coupled[t]).astype(BF16)
 
@@ -297,62 +325,84 @@
 
     first_halo = exchange(0, frozen, 2)
 
-    def spread(send, recv, s_sem, r_sem):
-        def step(k, carry):
-            peer = lax.rem(me + k, n)
-            pltpu.make_async_remote_copy(
-                src_ref=send.at[peer],
-                dst_ref=recv.at[k],
-                send_sem=s_sem.at[k],
-                recv_sem=r_sem.at[k],
-                device_id={"ta": peer},
-            ).start()
+    def remote(src, dst, send_sem, recv_sem, where):
+        return pltpu.make_async_remote_copy(
+            src_ref=src,
+            dst_ref=dst,
+            send_sem=send_sem,
+            recv_sem=recv_sem,
+            device_id={"ta": where},
+        )
+
+    def ahead(k):
+        return lax.rem(chip + k, chips)
+
+    def behind(k):
+        return lax.rem(chip + chips - k, chips)
+
+    def each(step):
+        def run(k, carry):
+            step(k)
             return carry
 
-        lax.fori_loop(1, n, step, 0)
-
-    def collect(send, recv, s_sem, r_sem):
+        lax.fori_loop(1, chips, run, 0)
+
+    def pair_copy(send, paired, sems):
+        return remote(send.at[other], paired, sems.at[0], sems.at[1], partner)
+
+    def load_send(send, packed):
+        rows = send.shape[2]
+        for p in range(n):
+            send[p // chips, p % chips] = packed[p * rows : (p + 1) * rows]
+
+    def pair_sum(send, paired):
+        paired[...] = (send[core].astype(F32) + paired[...].astype(F32)).astype(BF16)
+
+    def scatter_copy(paired, recv, s_sem, r_sem, k):
+        return remote(
+            paired.at[ahead(k)], recv.at[k], s_sem.at[k], r_sem.at[k], 2 * ahead(k) + core
+        )
+
+    def scatter(*refs):
+        each(lambda k: scatter_copy(*refs, k).start())
+
+    def collect(paired, recv, s_sem, r_sem):
         def step(k, total):
-            peer = lax.rem(me + k, n)
-            pltpu.make_async_remote_copy(
-                src_ref=send.at[peer],
-                dst_ref=recv.at[k],
-                send_sem=s_sem.at[k],
-                recv_sem=r_sem.at[k],
-                device_id={"ta": peer},
-            ).wait()
+            scatter_copy(paired, recv, s_sem, r_sem, k).wait()
             return total + recv[k].astype(F32)
 
-        return lax.fori_loop(1, n, step, send[me].astype(F32))
-
-    def share(buf, s_sem, r_sem):
-        def step(k, carry):
-            pltpu.make_async_remote_copy(
-                src_ref=buf.at[me],
-                dst_ref=buf.at[me],
-                send_sem=s_sem.at[k],
-                recv_sem=r_sem.at[k],
-                device_id={"ta": lax.rem(me + k, n)},
-            ).start()
-            return carry
-
-        lax.fori_loop(1, n, step, 0)
-
-    def share_done(buf, s_sem, r_sem):
-        def step(k, carry):
-            peer = lax.rem(me + n - k, n)
-            done = pltpu.make_async_remote_copy(
-                src_ref=buf.at[me],
-                dst_ref=buf.at[peer],
-                send_sem=s_sem.at[k],
-                recv_sem=r_sem.at[k],
-                device_id={"ta": lax.rem(me + k, n)},
-            )
-            done.wait_recv()
-            done.wait_send()
-            return carry
-
-        lax.fori_loop(1, n, step, 0)
+        return lax.fori_loop(1, chips, step, paired[chip].astype(F32)).astype(BF16)
+
+    def gather_copy(buf, s_sem, r_sem, k, at):
+        return remote(
+            buf.at[core, chip], buf.at[core, at], s_sem.at[k], r_sem.at[k], 2 * ahead(k) + core
+        )
+
+    def forward_copy(buf, f_send, f_recv, k, to):
+        return remote(
+            buf.at[core, behind(k)], buf.at[to, behind(k)], f_send.at[k], f_recv.at[k], partner
+        )
+
+    def gather(buf, s_sem, r_sem, f_send, f_recv):
+        forward_copy(buf, f_send, f_recv, 0, core).start()
+        each(lambda k: gather_copy(buf, s_sem, r_sem, k, chip).start())
+
+    def gather_forward(buf, s_sem, r_sem, f_send, f_recv):
+        def step(k):
+            gather_copy(buf, s_sem, r_sem, k, behind(k)).wait_recv()
+            forward_copy(buf, f_send, f_recv, k, core).start()
+
+        each(step)
+
+    def gather_done(buf, s_sem, r_sem, f_send, f_recv):
+        def step(k):
+            gather_copy(buf, s_sem, r_sem, k, chip).wait_send()
+            forward_copy(buf, f_send, f_recv, k, core).wait_send()
+            forward_copy(buf, f_send, f_recv, k, other).wait_recv()
+
+        forward_copy(buf, f_send, f_recv, 0, core).wait_send()
+        forward_copy(buf, f_send, f_recv, 0, other).wait_recv()
+        each(step)
 
     for kern, w, wt in ((kern1, w1, w1t), (kern2, w2, w2t)):
         ins = kern.shape[3]
@@ -362,10 +412,18 @@
         w[...] = wide.astype(BF16)
         wt[...] = wide.T.astype(BF16)
 
-    coupled_cot = [dot_tn(mixer, out_cot[:, t, :], HIGH) for t in range(count)]
+    cot_pieces = [split3(out_cot[:, t, :]) for t in range(count)]
+    coupled_cot = [mix_field(mixer_t, cot_pieces[t]) for t in range(count)]
+    wide_mix = None
+    for t in range(count):
+        term = dot_nt(
+            jnp.concatenate(cot_pieces[t], axis=0),
+            jnp.concatenate(split3(coupled[t]), axis=0),
+        )
+        wide_mix = term if wide_mix is None else wide_mix + term
     mix = None
-    for t in range(count):
-        term = dot_nt(out_cot[:, t, :], coupled[t], HIGH)
+    for i, j in ((2, 0), (1, 1), (0, 2), (1, 0), (0, 1), (0, 0)):
+        term = wide_mix[i * chans : (i + 1) * chans, j * chans : (j + 1) * chans]
         mix = term if mix is None else mix + term
     jac_sum = jnp.sum(jnp.sum(jac[...], axis=1, keepdims=True), axis=0, keepdims=True)
 
@@ -415,9 +473,9 @@
     packed2 = jnp.concatenate(
         [packed2, jnp.zeros((n * rows2 - total2, 128), F32)], axis=0
     ).astype(BF16)
-    for p in range(n):
-        send2[p] = packed2[p * rows2 : (p + 1) * rows2]
-    spread(send2, recv2, s2_send, s2_recv)
+    load_send(send2, packed2)
+    pair2 = pair_copy(send2, paired2, p2_sem)
+    pair2.start()
 
     ones = jnp.ones((8, sites), BF16)
     bias2_row = sum(dot_nt(ones, c) for c in cots)
@@ -434,38 +492,46 @@
         pres.append(pre)
     third_halo = exchange(4, pcot, 1)
 
+    pair2.wait()
+    pair_sum(send2, paired2)
+    scatter(paired2, recv2, s2_send, s2_recv)
+
     grads1 = kernel_grads(pres, lambda s: stack1[s + 2], count)
     total1, rows1 = block_rows(9 * hid, 9 * chans, FOLD1, n)
     packed1 = to_blocks(grads1, FOLD1)
     packed1 = jnp.concatenate(
         [packed1, jnp.zeros((n * rows1 - total1, 128), F32)], axis=0
     ).astype(BF16)
-    for p in range(n):
-        send1[p] = packed1[p * rows1 : (p + 1) * rows1]
-    spread(send1, recv1, s1_send, s1_recv)
+    load_send(send1, packed1)
+    pair1 = pair_copy(send1, paired1, p1_sem)
+    pair1.start()
 
     bias1_row = sum(dot_nt(ones, c) for c in pres)
     small_mine[...] = jnp.concatenate(
         [mix[:8], mix[8:], bias1_row, bias2_row, jnp.broadcast_to(jac_sum, (8, 32))], axis=1
     )
-
-    def small_copy(k):
-        return pltpu.make_async_remote_copy(
-            src_ref=small_mine,
-            dst_ref=small_all.at[k],
-            send_sem=sm_send.at[k],
-            recv_sem=sm_recv.at[k],
-            device_id={"ta": lax.rem(me + k, n)},
-        )
-
-    def small_start(k, carry):
-        small_copy(k).start()
-        return carry
-
-    lax.fori_loop(1, n, small_start, 0)
-
-    gath2[me] = collect(send2, recv2, s2_send, s2_recv).astype(BF16)
-    share(gath2, g2_send, g2_recv)
+    pair_small = remote(small_mine, small_other, ps_sem.at[0], ps_sem.at[1], partner)
+    pair_small.start()
+
+    pair1.wait()
+    pair_sum(send1, paired1)
+    scatter(paired1, recv1, s1_send, s1_recv)
+    pair_small.wait()
+    small_all[chip] = small_mine[...] + small_other[...]
+
+    def small_copy(k, at):
+        return remote(
+            small_all.at[chip],
+            small_all.at[at],
+            sm_send.at[k],
+            sm_recv.at[k],
+            2 * ahead(k) + core,
+        )
+
+    each(lambda k: small_copy(k, chip).start())
+
+    gath2[core, chip] = collect(paired2, recv2, s2_send, s2_recv)
+    gather(gath2, g2_send, g2_recv, f2_send, f2_recv)
 
     for copy in third_halo:
         copy.wait()
@@ -478,24 +544,24 @@
             keep[t] * (coupled_cot[t] + frozen_cot) + free * coupled_cot[t] * growth[t]
         )
 
-    gath1[me] = collect(send1, recv1, s1_send, s1_recv).astype(BF16)
-    share(gath1, g1_send, g1_recv)
-
-    def small_done(k, carry):
-        small_copy(k).wait()
-        return carry
-
-    lax.fori_loop(1, n, small_done, 0)
-    small_all[0] = small_mine[...]
-
-    def small_add(k, total):
-        return total + small_all[lax.rem(me + n - k, n)]
-
-    small_o[...] = lax.fori_loop(0, n, small_add, jnp.zeros(small_mine.shape, F32))
-
-    share_done(gath2, g2_send, g2_recv)
+    gath1[core, chip] = collect(paired1, recv1, s1_send, s1_recv)
+    gather(gath1, g1_send, g1_recv, f1_send, f1_recv)
+
+    gather_forward(gath2, g2_send, g2_recv, f2_send, f2_recv)
+
+    def small_done(k):
+        small_copy(k, chip).wait_send()
+        small_copy(k, behind(k)).wait_recv()
+
+    each(small_done)
+    small_o[...] = lax.fori_loop(
+        0, chips, lambda k, total: total + small_all[k], jnp.zeros(small_mine.shape, F32)
+    )
+
+    gather_forward(gath1, g1_send, g1_recv, f1_send, f1_recv)
+    gather_done(gath2, g2_send, g2_recv, f2_send, f2_recv)
     gath2_o[...] = gath2[...]
-    share_done(gath1, g1_send, g1_recv)
+    gather_done(gath1, g1_send, g1_recv, f1_send, f1_recv)
     gath1_o[...] = gath1[...]
 
 
@@ -565,6 +631,7 @@
 ):
     chans, count, sites = out_field.shape
     hid = kern1.shape[1]
+    chips = n // 2
     perm_row = perm.reshape(1, chans)
     log_row = log_scale.reshape(1, chans)
     _, rows1 = block_rows(9 * hid, 9 * chans, FOLD1, n)
@@ -578,8 +645,8 @@
         out_shape=(
             field,
             field,
-            shape((n, rows1, 128), BF16),
-            shape((n, rows2, 128), BF16),
+            shape((2, chips, rows1, 128), BF16),
+            shape((2, chips, rows2, 128), BF16),
             shape((8, 128), F32),
         ),
         in_specs=[vmem] * 12,
@@ -595,11 +662,15 @@
             pltpu.VMEM((9 * hid, 9 * hid), BF16),
             pltpu.VMEM((9 * hid, 9 * hid), BF16),
         ]
-        + [pltpu.VMEM((n, rows1, 128), BF16)] * 3
-        + [pltpu.VMEM((n, rows2, 128), BF16)] * 3
-        + [pltpu.VMEM((8, 128), F32), pltpu.VMEM((n, 8, 128), F32)]
+        + [pltpu.VMEM((2, chips, rows1, 128), BF16)] * 2
+        + [pltpu.VMEM((chips, rows1, 128), BF16)] * 2
+        + [pltpu.VMEM((2, chips, rows2, 128), BF16)] * 2
+        + [pltpu.VMEM((chips, rows2, 128), BF16)] * 2
+        + [pltpu.VMEM((8, 128), F32)] * 2
+        + [pltpu.VMEM((chips, 8, 128), F32)]
+        + [dma((2,))] * 3
         + [dma((6,))] * 2
-        + [dma((n,))] * 10,
+        + [dma((chips,))] * 14,
         compiler_params=pltpu.CompilerParams(
             collective_id=0, has_side_effects=True, vmem_limit_bytes=VMEM_LIMIT
         ),

time: 45.8 us -> 42.2 us (0.921)
  Pallas kernels: 37.5 us -> 33.8 us
    pallas_call x1, Pallas kernels: 36.2 us -> 32.5 us  [body(): pl.pallas_call(functools.partial(main_kernel, n), out_shape=(field, field...]
where the time goes in v1:
time: 42.2 us; the launch traced here: 42 us
  Pallas kernels  33.8 us (80%)
  local copies, waits for them, and re-layouts  7.34 us (17%)
  between operations  0.81 us (2%)
    pallas_call x1, Pallas kernels, body(): pl.pallas_call(functools.partial(main_kernel, n), out_shape=(field, field...  32.5 us
    unnamed x24, local copies, waits for them, and re-layouts  7.34 us
    pallas_call x1, Pallas kernels, body(): pl.pallas_call(functools.partial(last_kernel, norm), out_shape=(field, fi...  1.3 us

profile of v1, /device:TPU:0, one launch (start us, length us, event | category | flops | bytes accessed | tf_op | source)
XLA Modules:
  0.0 42.0 jit_solution(3369795260877202525)
XLA Ops:
  0.6 0.0 copy-start.3
  0.7 0.0 copy-start.2
  0.7 0.0 copy-start.9
  0.7 0.0 copy-start.8
  0.7 0.0 copy-start.7
  0.7 0.0 copy-start.6
  0.7 0.0 copy-start.5
  0.7 0.0 copy-start.4
  0.7 0.0 copy-start.1
  0.7 0.0 copy-start
  0.7 2.0 %copy.21 = bf16[81,32,16]{2,1,0:T(8,128)(2,1)S(1)} copy(bf16[81,32,16]{0,2,1:T(8,128)(2,1)} %param.20) | data formatting | bytes 165888 | tf_op args[8]
  2.8 2.0 %copy.22 = bf16[81,32,32]{2,1,0:T(8,128)(2,1)S(1)} copy(bf16[81,32,32]{0,2,1:T(8,128)(2,1)} %param.22) | data formatting | bytes 331776 | tf_op args[10]
  4.8 0.0 copy-done.3
  4.8 0.0 copy-done.2
  4.8 0.0 copy-done.9
  4.8 0.0 copy-done.8
  4.8 0.0 copy-done.7
  4.8 0.0 copy-done.6
  4.9 0.0 copy-done.5
  4.9 0.0 copy-done.4
  4.9 0.0 copy-done.1
  4.9 0.0 copy-done
  4.9 32.5 %block_backward.1 = (f32[16,2,1024]{2,1,0:T(2,128)S(1)}, f32[16,2,1024]{2,1,0:T(2,128)S(1)}, bf16[2,8,32,128]{3,2,1,0:T(8,128)(2,1)S(1)}, bf16[2,8,64,128]{3,2,1,0:T(8,128)(2,1)S(1)}, f32[8,128]{1,0:T(8,128)S(1)}) custom-call(f32[16,2,1024]{2,1,0:T(2,128)S(1)} %copy-done, f32[16,2,1024]{2,1,0:T(2,128)S(1)} %copy-done.1, f32[2,1024]{1,0:T(2,128)S(1)} %copy-done.4, ...), custom_call_target="tpu_custom_call" | custom-call | tf_op jit(solution)/shard_map/block_backward/pallas_call | solution.py:643
  37.4 1.3 %unpack.1 = (f32[16,2,1024]{2,1,0:T(2,128)}, f32[16,2,1024]{2,1,0:T(2,128)}, f32[9,9,32,16]{3,2,1,0:T(8,128)S(1)}, f32[1,32]{1,0:T(1,128)}, f32[9,9,32,32]{3,2,1...) custom-call(f32[16,2,1024]{2,1,0:T(2,128)S(1)} %get-tuple-element.23.field_in, ...), custom_call_target="tpu_custom_call" | custom-call | tf_op jit(solution)/shard_map/unpack/pallas_call | solution.py:693
  38.7 1.6 %copy.23 = f32[81,32,16]{0,2,1:T(8,128)} copy(f32[81,32,16]{2,1,0:T(8,128)S(1)} %bitcast.16) | data formatting | bytes 331776
  40.3 1.7 %copy.24 = f32[81,32,32]{0,2,1:T(8,128)} copy(f32[81,32,32]{2,1,0:T(8,128)S(1)} %bitcast.15) | data formatting | bytes 663552
Async XLA Ops:
  0.6 4.2 %copy-start.3 = (f32[16,16]{1,0:T(8,128)S(1)}, f32[16,16]{1,0:T(8,128)}, u32[]{:S(2)}) copy-start(f32[16,16]{1,0:T(8,128)} %upper.3) | copy-start | bytes 3076
  0.7 4.2 %copy-start.2 = (f32[16,16]{1,0:T(8,128)S(1)}, f32[16,16]{1,0:T(8,128)}, u32[]{:S(2)}) copy-start(f32[16,16]{1,0:T(8,128)} %lower.3) | copy-start | bytes 3076
  0.7 4.2 %copy-start.9 = (f32[32]{0:T(128)S(1)}, f32[32]{0:T(128)}, u32[]{:S(2)}) copy-start(f32[32]{0:T(128)} %param.23) | copy-start | bytes 388
  0.7 4.2 %copy-start.8 = (f32[32]{0:T(128)S(1)}, f32[32]{0:T(128)}, u32[]{:S(2)}) copy-start(f32[32]{0:T(128)} %param.21) | copy-start | bytes 388
  0.7 4.2 %copy-start.7 = (f32[16]{0:T(128)S(1)}, f32[16]{0:T(128)}, u32[]{:S(2)}) copy-start(f32[16]{0:T(128)} %param.19) | copy-start | bytes 196
  0.7 4.2 %copy-start.6 = (s32[16]{0:T(128)S(1)}, s32[16]{0:T(128)}, u32[]{:S(2)}) copy-start(s32[16]{0:T(128)} %param.16) | copy-start | bytes 196
  0.7 4.2 %copy-start.5 = (s32[2,1024]{1,0:T(2,128)S(1)}, s32[2,1024]{1,0:T(2,128)}, u32[]{:S(2)}) copy-start(s32[2,1024]{1,0:T(2,128)} %mask.1) | copy-start | bytes 24580
  0.7 4.2 %copy-start.4 = (f32[2,1024]{1,0:T(2,128)S(1)}, f32[2,1024]{1,0:T(2,128)}, u32[]{:S(2)}) copy-start(f32[2,1024]{1,0:T(2,128)} %jac.1) | copy-start | bytes 24580
  0.7 4.2 %copy-start.1 = (f32[16,2,1024]{2,1,0:T(2,128)S(1)}, f32[16,2,1024]{2,1,0:T(2,128)}, u32[]{:S(2)}) copy-start(f32[16,2,1024]{2,1,0:T(2,128)} %out_cot.1) | copy-start | bytes 393220
  0.7 4.2 %copy-start = (f32[16,2,1024]{2,1,0:T(2,128)S(1)}, f32[16,2,1024]{2,1,0:T(2,128)}, u32[]{:S(2)}) copy-start(f32[16,2,1024]{2,1,0:T(2,128)} %out_field.1) | copy-start | bytes 393220

commit v2 on v1

--- a/solution.py
+++ b/solution.py
@@ -61,17 +61,10 @@
     return jnp.sum(jnp.where(same, row, 0.0), axis=1, keepdims=True)
 
 
-def nilpotent_inverse(nilpart):
-    count = nilpart.shape[0]
-    eye = jnp.where(iota((count, count), 0) == iota((count, count), 1), 1.0, 0.0)
-    result = eye - nilpart
-    power = dot(nilpart, nilpart, HIGH)
-    span = 2
-    while span < count:
-        result = dot(result, eye + power, HIGH)
-        power = dot(power, power, HIGH)
-        span = span * 2
-    return result
+def substitute(strict, values, order):
+    for j in order:
+        values = values - strict[:, j : j + 1] * values[j : j + 1, :]
+    return values
 
 
 def factors(perm_row, lower_param, upper_param, log_row):
@@ -241,6 +234,8 @@
     w1t,
     w2,
     w2t,
+    taps1,
+    taps2,
     send1,
     gath1,
     paired1,
@@ -274,7 +269,7 @@
 ):
     me = lax.axis_index("ta")
     chans, count, sites = out_field.shape
-    hid = kern1.shape[2]
+    hid = kern1.shape[0]
     right, left = lax.rem(me + 1, n), lax.rem(me + n - 1, n)
     chips = n // 2
     chip, core = me // 2, lax.rem(me, 2)
@@ -292,10 +287,8 @@
     strict_low, strict_up, lower_tri, upper_tri, perm_t, diag = factors(
         perm[...], lower[...], upper[...], logs[...]
     )
-    inv_diag_row = jnp.exp(logs[...])
-    upper_inv = nilpotent_inverse(strict_up / diag) * (1.0 / inv_diag_row)
-    lower_inv = nilpotent_inverse(strict_low)
-    unmixer = dot(dot(upper_inv, lower_inv, HIGH), perm_t, HIGH)
+    solved = substitute(strict_low, perm_t, range(chans))
+    unmixer = substitute(strict_up / diag, solved / diag, range(chans - 1, -1, -1))
     mixer_t = dot_tn(dot(lower_tri, upper_tri, HIGH), perm_t, HIGH)
 
     keep = [mask[t : t + 1, :].astype(F32) for t in range(count)]
@@ -404,10 +397,14 @@
         forward_copy(buf, f_send, f_recv, 0, other).wait_recv()
         each(step)
 
-    for kern, w, wt in ((kern1, w1, w1t), (kern2, w2, w2t)):
-        ins = kern.shape[3]
+    for kern, taps, w, wt in ((kern1, taps1, w1, w1t), (kern2, taps2, w2, w2t)):
+        ins = kern.shape[1]
+        flat = kern[...].astype(F32).reshape(hid * ins, 81).T
+        for o in range(hid):
+            taps[pl.ds(o, 81, stride=hid), :] = flat[:, o * ins : (o + 1) * ins]
+        split = taps[...].reshape(9, 9, hid, ins)
         wide = jnp.concatenate(
-            [kern[:, k].astype(F32).reshape(9 * hid, ins) for k in range(9)], axis=1
+            [split[:, k].reshape(9 * hid, ins) for k in range(9)], axis=1
         )
         w[...] = wide.astype(BF16)
         wt[...] = wide.T.astype(BF16)
@@ -585,14 +582,25 @@
     lower_o,
     upper_o,
     logs_o,
+    taps1,
+    taps2,
 ):
     field_in_o[...] = field_in[...]
     field_cot_o[...] = field_cot[...]
-    for gath, out, fold in ((gath1, kern1_o, FOLD1), (gath2, kern2_o, FOLD2)):
-        hid, ins = out.shape[2], out.shape[3]
+    for gath, out, taps, fold in (
+        (gath1, kern1_o, taps1, FOLD1),
+        (gath2, kern2_o, taps2, FOLD2),
+    ):
+        hid, ins = out.shape[0], out.shape[1]
         grid = from_blocks(gath[...].astype(F32) * norm, 9 * hid, 9 * ins, fold)
         for k in range(9):
-            out[:, k] = grid[:, k * ins : (k + 1) * ins].reshape(9, hid, ins)
+            for x in range(9):
+                start = (9 * x + k) * hid
+                taps[start : start + hid, :] = grid[
+                    x * hid : (x + 1) * hid, k * ins : (k + 1) * ins
+                ]
+        flat = jnp.concatenate([taps[pl.ds(o, 81, stride=hid), :] for o in range(hid)], axis=1)
+        out[...] = flat.T.reshape(hid, ins, 81)
     _, _, lower_tri, upper_tri, perm_t, _ = factors(
         perm[...], lower[...], upper[...], logs[...]
     )
@@ -661,6 +669,8 @@
             pltpu.VMEM((9 * chans, 9 * hid), BF16),
             pltpu.VMEM((9 * hid, 9 * hid), BF16),
             pltpu.VMEM((9 * hid, 9 * hid), BF16),
+            pltpu.VMEM((81 * hid, chans), F32),
+            pltpu.VMEM((81 * hid, hid), F32),
         ]
         + [pltpu.VMEM((2, chips, rows1, 128), BF16)] * 2
         + [pltpu.VMEM((chips, rows1, 128), BF16)] * 2
@@ -684,9 +694,9 @@
         lower_param,
         upper_param,
         log_row,
-        kern1.reshape(9, 9, hid, chans),
+        kern1.transpose(1, 2, 0),
         bias1.reshape(1, hid),
-        kern2.reshape(9, 9, kern2.shape[1], hid),
+        kern2.transpose(1, 2, 0),
         bias2.reshape(1, -1),
     )
     norm = 1.0 / math.sqrt(count * sites * n)
@@ -695,9 +705,9 @@
         out_shape=(
             field,
             field,
-            shape((9, 9, hid, chans), F32),
+            shape((hid, chans, 81), F32),
             shape((1, hid), F32),
-            shape((9, 9, 2 * chans, hid), F32),
+            shape((2 * chans, hid, 81), F32),
             shape((1, 2 * chans), F32),
             shape((chans, chans), F32),
             shape((chans, chans), F32),
@@ -705,6 +715,10 @@
         ),
         in_specs=[vmem] * 9,
         out_specs=(vmem,) * 9,
+        scratch_shapes=[
+            pltpu.VMEM((81 * hid, chans), F32),
+            pltpu.VMEM((162 * chans, hid), F32),
+        ],
         compiler_params=pltpu.CompilerParams(vmem_limit_bytes=VMEM_LIMIT),
         name="unpack",
     )(
@@ -721,9 +735,9 @@
     return (
         outs[0],
         outs[1],
-        outs[2].reshape(81, hid, chans),
+        outs[2].transpose(2, 0, 1),
         outs[3].reshape(-1),
-        outs[4].reshape(81, 2 * chans, hid),
+        outs[4].transpose(2, 0, 1),
         outs[5].reshape(-1),
         outs[6],
         outs[7],

time: 42.2 us -> 43.7 us (1.036)
  Pallas kernels: 33.8 us -> 36.2 us
  local copies, waits for them, and re-layouts: 7.34 us -> 6.43 us
    pallas_call x1, Pallas kernels: 1.3 us -> 3.56 us  [body(): pl.pallas_call(functools.partial(last_kernel, norm), out_shape=(field, fi...]
    unnamed x24, local copies, waits for them, and re-layouts: 7.34 us -> 6.43 us
where the time goes in v2:
time: 43.7 us; the launch traced here: 43.3 us
  Pallas kernels  36.2 us (83%)
  local copies, waits for them, and re-layouts  6.43 us (15%)
  between operations  0.7 us (2%)
    pallas_call x1, Pallas kernels, body(): pl.pallas_call(functools.partial(main_kernel, n), out_shape=(field, field...  32.6 us
    unnamed x24, local copies, waits for them, and re-layouts  6.43 us
    pallas_call x1, Pallas kernels, body(): pl.pallas_call(functools.partial(last_kernel, norm), out_shape=(field, fi...  3.56 us

profile of v2, /device:TPU:0, one launch (start us, length us, event | category | flops | bytes accessed | tf_op | source)
XLA Modules:
  0.0 43.3 jit_solution(11090934769493339911)
XLA Ops:
  0.6 0.0 copy-start.4
  0.7 0.0 copy-start.11
  0.7 0.0 copy-start.8
  0.7 0.0 copy-start.9
  0.7 0.0 copy-start.10
  0.7 0.6 %copy-done.4 = f32[16,16]{1,0:T(8,128)S(1)} copy-done((f32[16,16]{1,0:T(8,128)S(1)}, f32[16,16]{1,0:T(8,128)}, u32[]{:S(2)}) %copy-start.4) | copy-done | bytes 1048
  1.3 0.0 copy-done.11
  1.3 0.0 copy-done.8
  1.4 0.0 copy-done.9
  1.4 0.0 copy-done.10
  1.4 0.0 copy-start
  1.4 0.9 %copy-done = bf16[81,32,32]{0,2,1:T(8,128)(2,1)S(1)} copy-done((bf16[81,32,32]{0,2,1:T(8,128)(2,1)S(1)}, bf16[81,32,32]{0,2,1:T(8,128)(2,1)}, u32[]{:S(2)}) %copy-start) | copy-done | bytes 165912
  2.3 0.0 copy-start.1
  2.3 0.9 %copy-done.1 = f32[16,2,1024]{2,1,0:T(2,128)S(1)} copy-done((f32[16,2,1024]{2,1,0:T(2,128)S(1)}, f32[16,2,1024]{2,1,0:T(2,128)}, u32[]{:S(2)}) %copy-start.1) | copy-done | bytes 131096
  3.2 0.0 copy-start.2
  3.2 0.9 %copy-done.2 = f32[16,2,1024]{2,1,0:T(2,128)S(1)} copy-done((f32[16,2,1024]{2,1,0:T(2,128)S(1)}, f32[16,2,1024]{2,1,0:T(2,128)}, u32[]{:S(2)}) %copy-start.2) | copy-done | bytes 131096
  4.1 0.0 copy-start.3
  4.1 0.9 %copy-done.3 = bf16[81,32,16]{0,2,1:T(8,128)(2,1)S(1)} copy-done((bf16[81,32,16]{0,2,1:T(8,128)(2,1)S(1)}, bf16[81,32,16]{0,2,1:T(8,128)(2,1)}, u32[]{:S(2)}) %copy-start.3) | copy-done | bytes 82968
  5.0 0.0 copy-start.5
  5.0 0.7 %copy-done.5 = f32[16,16]{1,0:T(8,128)S(1)} copy-done((f32[16,16]{1,0:T(8,128)S(1)}, f32[16,16]{1,0:T(8,128)}, u32[]{:S(2)}) %copy-start.5) | copy-done | bytes 1048
  5.7 0.0 copy-start.6
  5.7 0.7 %copy-done.6 = f32[2,1024]{1,0:T(2,128)S(1)} copy-done((f32[2,1024]{1,0:T(2,128)S(1)}, f32[2,1024]{1,0:T(2,128)}, u32[]{:S(2)}) %copy-start.6) | copy-done | bytes 8216
  6.4 0.0 copy-start.7
  6.4 0.7 %copy-done.7 = s32[2,1024]{1,0:T(2,128)S(1)} copy-done((s32[2,1024]{1,0:T(2,128)S(1)}, s32[2,1024]{1,0:T(2,128)}, u32[]{:S(2)}) %copy-start.7) | copy-done | bytes 8216
  7.1 32.6 %block_backward.1 = (f32[16,2,1024]{2,1,0:T(2,128)S(1)}, f32[16,2,1024]{2,1,0:T(2,128)S(1)}, bf16[2,8,32,128]{3,2,1,0:T(8,128)(2,1)S(1)}, bf16[2,8,64,128]{3,2,1,0:T(8,128)(2,1)S(1)}, f32[8,128]{1,0:T(8,128)S(1)}) custom-call(f32[16,2,1024]{2,1,0:T(2,128)S(1)} %copy-done.1, f32[16,2,1024]{2,1,0:T(2,128)S(1)} %copy-done.2, f32[2,1024]{1,0:T(2,128)S(1)} %copy-done.6, ...), custom_call_target="tpu_custom_call" | custom-call | tf_op jit(solution)/shard_map/block_backward/pallas_call | solution.py:651
  39.7 3.6 %unpack.1 = (f32[16,2,1024]{2,1,0:T(2,128)}, f32[16,2,1024]{2,1,0:T(2,128)}, f32[32,16,81]{2,1,0:T(8,128)}, f32[1,32]{1,0:T(1,128)}, f32[32,32,81]{2,1,0:T(8,128...) custom-call(f32[16,2,1024]{2,1,0:T(2,128)S(1)} %get-tuple-element.23.field_in, ...), custom_call_target="tpu_custom_call" | custom-call | tf_op jit(solution)/shard_map/unpack/pallas_call | solution.py:703
Async XLA Ops:
  0.6 0.7 %copy-start.4 = (f32[16,16]{1,0:T(8,128)S(1)}, f32[16,16]{1,0:T(8,128)}, u32[]{:S(2)}) copy-start(f32[16,16]{1,0:T(8,128)} %lower.3) | copy-start | bytes 3076
  0.7 0.7 %copy-start.11 = (f32[32]{0:T(128)S(1)}, f32[32]{0:T(128)}, u32[]{:S(2)}) copy-start(f32[32]{0:T(128)} %param.23) | copy-start | bytes 388
  0.7 0.7 %copy-start.8 = (s32[16]{0:T(128)S(1)}, s32[16]{0:T(128)}, u32[]{:S(2)}) copy-start(s32[16]{0:T(128)} %param.16) | copy-start | bytes 196
  0.7 0.7 %copy-start.9 = (f32[16]{0:T(128)S(1)}, f32[16]{0:T(128)}, u32[]{:S(2)}) copy-start(f32[16]{0:T(128)} %param.19) | copy-start | bytes 196
  0.7 0.7 %copy-start.10 = (f32[32]{0:T(128)S(1)}, f32[32]{0:T(128)}, u32[]{:S(2)}) copy-start(f32[32]{0:T(128)} %param.21) | copy-start | bytes 388
  1.4 0.9 %copy-start = (bf16[81,32,32]{0,2,1:T(8,128)(2,1)S(1)}, bf16[81,32,32]{0,2,1:T(8,128)(2,1)}, u32[]{:S(2)}) copy-start(bf16[81,32,32]{0,2,1:T(8,128)(2,1)} %param.22) | copy-start | bytes 497668
  2.3 0.9 %copy-start.1 = (f32[16,2,1024]{2,1,0:T(2,128)S(1)}, f32[16,2,1024]{2,1,0:T(2,128)}, u32[]{:S(2)}) copy-start(f32[16,2,1024]{2,1,0:T(2,128)} %out_field.1) | copy-start | bytes 393220
  3.2 0.9 %copy-start.2 = (f32[16,2,1024]{2,1,0:T(2,128)S(1)}, f32[16,2,1024]{2,1,0:T(2,128)}, u32[]{:S(2)}) copy-start(f32[16,2,1024]{2,1,0:T(2,128)} %out_cot.1) | copy-start | bytes 393220
  4.1 0.9 %copy-start.3 = (bf16[81,32,16]{0,2,1:T(8,128)(2,1)S(1)}, bf16[81,32,16]{0,2,1:T(8,128)(2,1)}, u32[]{:S(2)}) copy-start(bf16[81,32,16]{0,2,1:T(8,128)(2,1)} %param.20) | copy-start | bytes 248836
  5.0 0.7 %copy-start.5 = (f32[16,16]{1,0:T(8,128)S(1)}, f32[16,16]{1,0:T(8,128)}, u32[]{:S(2)}) copy-start(f32[16,16]{1,0:T(8,128)} %upper.3) | copy-start | bytes 3076
  5.7 0.7 %copy-start.6 = (f32[2,1024]{1,0:T(2,128)S(1)}, f32[2,1024]{1,0:T(2,128)}, u32[]{:S(2)}) copy-start(f32[2,1024]{1,0:T(2,128)} %jac.1) | copy-start | bytes 24580
  6.4 0.7 %copy-start.7 = (s32[2,1024]{1,0:T(2,128)S(1)}, s32[2,1024]{1,0:T(2,128)}, u32[]{:S(2)}) copy-start(s32[2,1024]{1,0:T(2,128)} %mask.1) | copy-start | bytes 24580

commit v3 on v2

--- a/solution.py
+++ b/solution.py
@@ -16,7 +16,7 @@
 HIGH = lax.Precision.HIGHEST
 F32 = jnp.float32
 BF16 = jnp.bfloat16
-VMEM_LIMIT = 48 * 1024 * 1024
+VMEM_LIMIT = 63 * 1024 * 1024
 
 
 def dot(a, b, precision=None):
@@ -206,8 +206,35 @@
 FOLD2 = 1
 
 
-def main_kernel(
+def unpack_grad(packed, taps, hid, ins, fold, norm):
+    grid = from_blocks(packed.astype(F32) * norm, 9 * hid, 9 * ins, fold)
+    for k in range(9):
+        for x in range(9):
+            start = (9 * x + k) * hid
+            taps[start : start + hid, :] = grid[
+                x * hid : (x + 1) * hid, k * ins : (k + 1) * ins
+            ]
+    flat = jnp.concatenate([taps[pl.ds(o, 81, stride=hid), :] for o in range(hid)], axis=1)
+    return flat.T.reshape(hid, ins, 81)
+
+
+def main_kernel(n, norm, *refs):
+    given, refs = refs[:12], refs[12:]
+    held, rest = refs[5:17], refs[:5] + refs[17:-1]
+    in_sem = refs[-1]
+    loads = [
+        pltpu.make_async_copy(src, dst, in_sem.at[i])
+        for i, (src, dst) in enumerate(zip(given, held))
+    ]
+    for i in (5, 6, 7, 4, 0, 3, 8, 10, 1, 2, 9, 11):
+        loads[i].start()
+    compute(n, norm, loads, *held, *rest)
+
+
+def compute(
     n,
+    norm,
+    loads,
     out_field,
     out_cot,
     jac,
@@ -223,7 +250,7 @@
     field_in_o,
     field_cot_o,
     gath1_o,
-    gath2_o,
+    kern2_o,
     small_o,
     frozen,
     stack1,
@@ -284,6 +311,8 @@
 
     lax.fori_loop(1, n, greet, 0)
 
+    for i in (4, 5, 6, 7):
+        loads[i].wait()
     strict_low, strict_up, lower_tri, upper_tri, perm_t, diag = factors(
         perm[...], lower[...], upper[...], logs[...]
     )
@@ -291,6 +320,8 @@
     unmixer = substitute(strict_up / diag, solved / diag, range(chans - 1, -1, -1))
     mixer_t = dot_tn(dot(lower_tri, upper_tri, HIGH), perm_t, HIGH)
 
+    for i in (0, 3):
+        loads[i].wait()
     keep = [mask[t : t + 1, :].astype(F32) for t in range(count)]
     coupled = [mix_field(unmixer, split3(out_field[:, t, :])) for t in range(count)]
     for t in range(count):
@@ -397,6 +428,8 @@
         forward_copy(buf, f_send, f_recv, 0, other).wait_recv()
         each(step)
 
+    for i in (8, 10, 1, 2, 9, 11):
+        loads[i].wait()
     for kern, taps, w, wt in ((kern1, taps1, w1, w1t), (kern2, taps2, w2, w2t)):
         ins = kern.shape[1]
         flat = kern[...].astype(F32).reshape(hid * ins, 81).T
@@ -545,6 +578,10 @@
     gather(gath1, g1_send, g1_recv, f1_send, f1_recv)
 
     gather_forward(gath2, g2_send, g2_recv, f2_send, f2_recv)
+    gather_done(gath2, g2_send, g2_recv, f2_send, f2_recv)
+    kern2_o[...] = unpack_grad(
+        gath2[...].reshape(n * rows2, 128), taps2, hid, hid, FOLD2, norm
+    )
 
     def small_done(k):
         small_copy(k, chip).wait_send()
@@ -556,8 +593,6 @@
     )
 
     gather_forward(gath1, g1_send, g1_recv, f1_send, f1_recv)
-    gather_done(gath2, g2_send, g2_recv, f2_send, f2_recv)
-    gath2_o[...] = gath2[...]
     gather_done(gath1, g1_send, g1_recv, f1_send, f1_recv)
     gath1_o[...] = gath1[...]
 
@@ -567,7 +602,7 @@
     field_in,
     field_cot,
     gath1,
-    gath2,
+    kern2,
     small,
     perm,
     lower,
@@ -583,24 +618,18 @@
     upper_o,
     logs_o,
     taps1,
-    taps2,
+    out_sem,
 ):
-    field_in_o[...] = field_in[...]
-    field_cot_o[...] = field_cot[...]
-    for gath, out, taps, fold in (
-        (gath1, kern1_o, taps1, FOLD1),
-        (gath2, kern2_o, taps2, FOLD2),
-    ):
-        hid, ins = out.shape[0], out.shape[1]
-        grid = from_blocks(gath[...].astype(F32) * norm, 9 * hid, 9 * ins, fold)
-        for k in range(9):
-            for x in range(9):
-                start = (9 * x + k) * hid
-                taps[start : start + hid, :] = grid[
-                    x * hid : (x + 1) * hid, k * ins : (k + 1) * ins
-                ]
-        flat = jnp.concatenate([taps[pl.ds(o, 81, stride=hid), :] for o in range(hid)], axis=1)
-        out[...] = flat.T.reshape(hid, ins, 81)
+    moves = [
+        pltpu.make_async_copy(src, dst, out_sem.at[i])
+        for i, (src, dst) in enumerate(
+            ((kern2, kern2_o), (field_in, field_in_o), (field_cot, field_cot_o))
+        )
+    ]
+    for move in moves:
+        move.start()
+    hid, ins = kern1_o.shape[0], kern1_o.shape[1]
+    kern1_o[...] = unpack_grad(gath1[...], taps1, hid, ins, FOLD1, norm)
     _, _, lower_tri, upper_tri, perm_t, _ = factors(
         perm[...], lower[...], upper[...], logs[...]
     )
@@ -620,6 +649,8 @@
     diag = jnp.sum(jnp.where(rows == cols, upper_full, 0.0), axis=0, keepdims=True)
     jac_row = sums[0:1, base + 2 * hid : base + 2 * hid + chans]
     logs_o[...] = diag * jnp.exp(logs[...]) + jac_row
+    for move in moves:
+        move.wait()
 
 
 def body(
@@ -648,18 +679,32 @@
     shape = jax.ShapeDtypeStruct
     field = shape((chans, count, sites), F32)
     dma = pltpu.SemaphoreType.DMA
-    field_in, field_cot, gath1, gath2, small = pl.pallas_call(
-        functools.partial(main_kernel, n),
+    norm = 1.0 / math.sqrt(count * sites * n)
+    hbm = pl.BlockSpec(memory_space=pltpu.HBM)
+    field_in, field_cot, gath1, grad2, small = pl.pallas_call(
+        functools.partial(main_kernel, n, norm),
         out_shape=(
             field,
             field,
             shape((2, chips, rows1, 128), BF16),
-            shape((2, chips, rows2, 128), BF16),
+            shape((2 * chans, hid, 81), F32),
             shape((8, 128), F32),
         ),
-        in_specs=[vmem] * 12,
+        in_specs=[hbm] * 12,
         out_specs=(vmem,) * 5,
         scratch_shapes=[
+            pltpu.VMEM((chans, count, sites), F32),
+            pltpu.VMEM((chans, count, sites), F32),
+            pltpu.VMEM((count, sites), F32),
+            pltpu.VMEM((count, sites), jnp.int32),
+            pltpu.VMEM((1, chans), jnp.int32),
+            pltpu.VMEM((chans, chans), F32),
+            pltpu.VMEM((chans, chans), F32),
+            pltpu.VMEM((1, chans), F32),
+            pltpu.VMEM((hid, chans, 81), BF16),
+            pltpu.VMEM((1, hid), F32),
+            pltpu.VMEM((2 * chans, hid, 81), BF16),
+            pltpu.VMEM((1, 2 * chans), F32),
             pltpu.VMEM((count + 4, chans, sites), BF16),
             pltpu.VMEM((count + 4, 9 * chans, sites), BF16),
             pltpu.VMEM((count + 2, 9 * hid, sites), BF16),
@@ -680,7 +725,8 @@
         + [pltpu.VMEM((chips, 8, 128), F32)]
         + [dma((2,))] * 3
         + [dma((6,))] * 2
-        + [dma((chips,))] * 14,
+        + [dma((chips,))] * 14
+        + [dma((12,))],
         compiler_params=pltpu.CompilerParams(
             collective_id=0, has_side_effects=True, vmem_limit_bytes=VMEM_LIMIT
         ),
@@ -699,7 +745,6 @@
         kern2.transpose(1, 2, 0),
         bias2.reshape(1, -1),
     )
-    norm = 1.0 / math.sqrt(count * sites * n)
     outs = pl.pallas_call(
         functools.partial(last_kernel, norm),
         out_shape=(
@@ -714,18 +759,15 @@
             shape((1, chans), F32),
         ),
         in_specs=[vmem] * 9,
-        out_specs=(vmem,) * 9,
-        scratch_shapes=[
-            pltpu.VMEM((81 * hid, chans), F32),
-            pltpu.VMEM((162 * chans, hid), F32),
-        ],
+        out_specs=(hbm, hbm, vmem, vmem, hbm, vmem, vmem, vmem, vmem),
+        scratch_shapes=[pltpu.VMEM((81 * hid, chans), F32), dma((3,))],
         compiler_params=pltpu.CompilerParams(vmem_limit_bytes=VMEM_LIMIT),
         name="unpack",
     )(
         field_in,
         field_cot,
         gath1.reshape(n * rows1, 128),
-        gath2.reshape(n * rows2, 128),
+        grad2,
         small,
         perm_row,
         lower_param,

time: 43.7 us -> 39.2 us (0.90)
  local copies, waits for them, and re-layouts: 6.43 us -> 0 us
  Pallas kernels: 36.2 us -> 38.4 us
    unnamed x24 -> x0, local copies, waits for them, and re-layouts: 6.43 us -> none
    pallas_call x1, Pallas kernels: 32.6 us -> 35 us  [body(): pl.pallas_call(functools.partial(main_kernel, n, norm), out_shape=(field,...]
where the time goes in v3:
time: 39.2 us; the launch traced here: 39 us
  Pallas kernels  38.4 us (98%)
  between operations  0.65 us (2%)
    pallas_call x1, Pallas kernels, body(): pl.pallas_call(functools.partial(main_kernel, n, norm), out_shape=(field,...  35 us
    pallas_call x1, Pallas kernels, body(): pl.pallas_call(functools.partial(last_kernel, norm), out_shape=(field, fi...  3.33 us

profile of v3, /device:TPU:0, one launch (start us, length us, event | category | flops | bytes accessed | tf_op | source)
XLA Modules:
  0.0 39.0 jit_solution(3054382085256117914)
XLA Ops:
  0.6 35.0 %block_backward.1 = (f32[16,2,1024]{2,1,0:T(2,128)}, f32[16,2,1024]{2,1,0:T(2,128)}, bf16[2,8,32,128]{3,2,1,0:T(8,128)(2,1)}, f32[32,32,81]{2,1,0:T(8,128)}, f32[8,128]{1,0:T(8,128)}) custom-call(f32[16,2,1024]{2,1,0:T(2,128)} %refs_0_.1, f32[16,2,1024]{2,1,0:T(2,128)} %refs_1_.1, f32[2,1024]{1,0:T(2,128)} %refs_2_.1, s32[2,1024]{1,0:T(2,128)} %refs_3_.1, ...), custom_call_target="tpu_custom_call" | custom-call | tf_op jit(solution)/shard_map/block_backward/pallas_call | solution.py:684
  35.7 3.3 %unpack.1 = (f32[16,2,1024]{2,1,0:T(2,128)}, f32[16,2,1024]{2,1,0:T(2,128)}, f32[32,16,81]{2,1,0:T(8,128)}, f32[1,32]{1,0:T(1,128)}, f32[32,32,81]{2,1,0:T(8,128...) custom-call(f32[16,2,1024]{2,1,0:T(2,128)} %get-tuple-element.23.field_in, ...), custom_call_target="tpu_custom_call" | custom-call | tf_op jit(solution)/shard_map/unpack/pallas_call | solution.py:748

commit v4 on v3

--- a/solution.py
+++ b/solution.py
@@ -202,12 +202,15 @@
     return total, 16 * -(-blocks // n)
 
 
-FOLD1 = 3
 FOLD2 = 1
 
 
 def unpack_grad(packed, taps, hid, ins, fold, norm):
     grid = from_blocks(packed.astype(F32) * norm, 9 * hid, 9 * ins, fold)
+    return tap_rows(grid, taps, hid, ins).reshape(hid, ins, 81)
+
+
+def tap_rows(grid, taps, hid, ins):
     for k in range(9):
         for x in range(9):
             start = (9 * x + k) * hid
@@ -215,12 +218,12 @@
                 x * hid : (x + 1) * hid, k * ins : (k + 1) * ins
             ]
     flat = jnp.concatenate([taps[pl.ds(o, 81, stride=hid), :] for o in range(hid)], axis=1)
-    return flat.T.reshape(hid, ins, 81)
+    return flat.T
 
 
 def main_kernel(n, norm, *refs):
     given, refs = refs[:12], refs[12:]
-    held, rest = refs[5:17], refs[:5] + refs[17:-1]
+    held, rest = refs[9:21], refs[:9] + refs[21:-1]
     in_sem = refs[-1]
     loads = [
         pltpu.make_async_copy(src, dst, in_sem.at[i])
@@ -249,9 +252,13 @@
     bias2,
     field_in_o,
     field_cot_o,
-    gath1_o,
+    kern1_o,
+    bias1_o,
     kern2_o,
-    small_o,
+    bias2_o,
+    lower_o,
+    upper_o,
+    logs_o,
     frozen,
     stack1,
     stack2,
@@ -527,11 +534,14 @@
     scatter(paired2, recv2, s2_send, s2_recv)
 
     grads1 = kernel_grads(pres, lambda s: stack1[s + 2], count)
-    total1, rows1 = block_rows(9 * hid, 9 * chans, FOLD1, n)
-    packed1 = to_blocks(grads1, FOLD1)
-    packed1 = jnp.concatenate(
-        [packed1, jnp.zeros((n * rows1 - total1, 128), F32)], axis=0
-    ).astype(BF16)
+    rows1 = send1.shape[2]
+    ordered = tap_rows(grads1, taps1, hid, chans)
+    packed1 = jnp.concatenate([ordered, jnp.zeros((hid * chans, 47), F32)], axis=1)
+    if n * rows1 > hid * chans:
+        packed1 = jnp.concatenate(
+            [packed1, jnp.zeros((n * rows1 - hid * chans, 128), F32)], axis=0
+        )
+    packed1 = packed1.astype(BF16)
     load_send(send1, packed1)
     pair1 = pair_copy(send1, paired1, p1_sem)
     pair1.start()
@@ -542,6 +552,9 @@
     )
     pair_small = remote(small_mine, small_other, ps_sem.at[0], ps_sem.at[1], partner)
     pair_small.start()
+
+    gath2[core, chip] = collect(paired2, recv2, s2_send, s2_recv)
+    gather(gath2, g2_send, g2_recv, f2_send, f2_recv)
 
     pair1.wait()
     pair_sum(send1, paired1)
@@ -559,9 +572,6 @@
         )
 
     each(lambda k: small_copy(k, chip).start())
-
-    gath2[core, chip] = collect(paired2, recv2, s2_send, s2_recv)
-    gather(gath2, g2_send, g2_recv, f2_send, f2_recv)
 
     for copy in third_halo:
         copy.wait()
@@ -588,59 +598,16 @@
         small_copy(k, behind(k)).wait_recv()
 
     each(small_done)
-    small_o[...] = lax.fori_loop(
+    small_sum = lax.fori_loop(
         0, chips, lambda k, total: total + small_all[k], jnp.zeros(small_mine.shape, F32)
     )
 
-    gather_forward(gath1, g1_send, g1_recv, f1_send, f1_recv)
-    gather_done(gath1, g1_send, g1_recv, f1_send, f1_recv)
-    gath1_o[...] = gath1[...]
-
-
-def last_kernel(
-    norm,
-    field_in,
-    field_cot,
-    gath1,
-    kern2,
-    small,
-    perm,
-    lower,
-    upper,
-    logs,
-    field_in_o,
-    field_cot_o,
-    kern1_o,
-    bias1_o,
-    kern2_o,
-    bias2_o,
-    lower_o,
-    upper_o,
-    logs_o,
-    taps1,
-    out_sem,
-):
-    moves = [
-        pltpu.make_async_copy(src, dst, out_sem.at[i])
-        for i, (src, dst) in enumerate(
-            ((kern2, kern2_o), (field_in, field_in_o), (field_cot, field_cot_o))
-        )
-    ]
-    for move in moves:
-        move.start()
-    hid, ins = kern1_o.shape[0], kern1_o.shape[1]
-    kern1_o[...] = unpack_grad(gath1[...], taps1, hid, ins, FOLD1, norm)
-    _, _, lower_tri, upper_tri, perm_t, _ = factors(
-        perm[...], lower[...], upper[...], logs[...]
-    )
-    sums = small[...] * norm
-    chans = lower.shape[0]
-    hid = bias1_o.shape[1]
-    mix = jnp.concatenate([sums[:, :chans], sums[:, chans : 2 * chans]], axis=0)
+    sums = small_sum * norm
+    total_mix = jnp.concatenate([sums[:, :chans], sums[:, chans : 2 * chans]], axis=0)
     base = 2 * chans
     bias1_o[...] = sums[0:1, base : base + hid]
     bias2_o[...] = sums[0:1, base + hid : base + 2 * hid]
-    turned = dot(perm_t, mix, HIGH)
+    turned = dot(perm_t, total_mix, HIGH)
     lower_full = dot_nt(turned, upper_tri, HIGH)
     upper_full = dot_tn(lower_tri, turned, HIGH)
     rows, cols = iota((chans, chans), 0), iota((chans, chans), 1)
@@ -649,6 +616,20 @@
     diag = jnp.sum(jnp.where(rows == cols, upper_full, 0.0), axis=0, keepdims=True)
     jac_row = sums[0:1, base + 2 * hid : base + 2 * hid + chans]
     logs_o[...] = diag * jnp.exp(logs[...]) + jac_row
+
+    gather_forward(gath1, g1_send, g1_recv, f1_send, f1_recv)
+    gather_done(gath1, g1_send, g1_recv, f1_send, f1_recv)
+    done1 = gath1[...].reshape(n * rows1, 128)[: hid * chans, :81].astype(F32) * norm
+    kern1_o[...] = done1.reshape(hid, chans, 81)
+
+
+def last_kernel(*refs):
+    out_sem = refs[18]
+    moves = [
+        pltpu.make_async_copy(refs[i], refs[9 + i], out_sem.at[i]) for i in range(9)
+    ]
+    for i in (4, 2, 0, 1, 3, 5, 6, 7, 8):
+        moves[i].start()
     for move in moves:
         move.wait()
 
@@ -673,7 +654,7 @@
     chips = n // 2
     perm_row = perm.reshape(1, chans)
     log_row = log_scale.reshape(1, chans)
-    _, rows1 = block_rows(9 * hid, 9 * chans, FOLD1, n)
+    rows1 = 16 * -(-(hid * chans // 16) // n)
     _, rows2 = block_rows(9 * hid, 9 * hid, FOLD2, n)
     vmem = pl.BlockSpec(memory_space=pltpu.VMEM)
     shape = jax.ShapeDtypeStruct
@@ -681,17 +662,22 @@
     dma = pltpu.SemaphoreType.DMA
     norm = 1.0 / math.sqrt(count * sites * n)
     hbm = pl.BlockSpec(memory_space=pltpu.HBM)
-    field_in, field_cot, gath1, grad2, small = pl.pallas_call(
+    results = (
+        field,
+        field,
+        shape((hid, chans, 81), F32),
+        shape((1, hid), F32),
+        shape((2 * chans, hid, 81), F32),
+        shape((1, 2 * chans), F32),
+        shape((chans, chans), F32),
+        shape((chans, chans), F32),
+        shape((1, chans), F32),
+    )
+    found = pl.pallas_call(
         functools.partial(main_kernel, n, norm),
-        out_shape=(
-            field,
-            field,
-            shape((2, chips, rows1, 128), BF16),
-            shape((2 * chans, hid, 81), F32),
-            shape((8, 128), F32),
-        ),
+        out_shape=results,
         in_specs=[hbm] * 12,
-        out_specs=(vmem,) * 5,
+        out_specs=(vmem,) * 9,
         scratch_shapes=[
             pltpu.VMEM((chans, count, sites), F32),
             pltpu.VMEM((chans, count, sites), F32),
@@ -746,34 +732,14 @@
         bias2.reshape(1, -1),
     )
     outs = pl.pallas_call(
-        functools.partial(last_kernel, norm),
-        out_shape=(
-            field,
-            field,
-            shape((hid, chans, 81), F32),
-            shape((1, hid), F32),
-            shape((2 * chans, hid, 81), F32),
-            shape((1, 2 * chans), F32),
-            shape((chans, chans), F32),
-            shape((chans, chans), F32),
-            shape((1, chans), F32),
-        ),
-        in_specs=[vmem] * 9,
-        out_specs=(hbm, hbm, vmem, vmem, hbm, vmem, vmem, vmem, vmem),
-        scratch_shapes=[pltpu.VMEM((81 * hid, chans), F32), dma((3,))],
+        last_kernel,
+        out_shape=results,
+        in_specs=[hbm] * 9,
+        out_specs=(hbm,) * 9,
+        scratch_shapes=[dma((9,))],
         compiler_params=pltpu.CompilerParams(vmem_limit_bytes=VMEM_LIMIT),
-        name="unpack",
-    )(
-        field_in,
-        field_cot,
-        gath1.reshape(n * rows1, 128),
-        grad2,
-        small,
-        perm_row,
-        lower_param,
-        upper_param,
-        log_row,
-    )
+        name="deliver",
+    )(*found)
     return (
         outs[0],
         outs[1],

time: 39.2 us -> 72.6 us (1.85)
  Pallas kernels: 38.4 us -> 71.8 us
    pallas_call x2, Pallas kernels: 38.4 us -> 71.8 us  [the longest x1 38.3 us: body(): pl.pallas_call(functools.partial(main_kernel, n, norm), out_shape=results...]
where the time goes in v4:
time: 72.6 us; the launch traced here: 72.4 us
  Pallas kernels  71.8 us (99%)
    pallas_call x1, Pallas kernels, body(): pl.pallas_call(functools.partial(main_kernel, n, norm), out_shape=results...  38.3 us
    pallas_call x1, Pallas kernels, body(): pl.pallas_call(last_kernel, out_shape=results, in_specs=[hbm] * 9, out_sp...  33.5 us

profile of v4, /device:TPU:0, one launch (start us, length us, event | category | flops | bytes accessed | tf_op | source)
XLA Modules:
  0.0 72.4 jit_solution(4993095087783003745)
XLA Ops:
  0.6 38.3 %block_backward.1 = (f32[16,2,1024]{2,1,0:T(2,128)}, f32[16,2,1024]{2,1,0:T(2,128)}, f32[32,16,81]{2,1,0:T(8,128)}, f32[1,32]{1,0:T(1,128)}, f32[32,32,81]{2,1,0...) custom-call(f32[16,2,1024]{2,1,0:T(2,128)} %refs_0_.1, ...), custom_call_target="tpu_custom_call" | custom-call | tf_op jit(solution)/shard_map/block_backward/pallas_call | solution.py:676
  38.9 33.5 %deliver.1 = (f32[16,2,1024]{2,1,0:T(2,128)}, f32[16,2,1024]{2,1,0:T(2,128)}, f32[32,16,81]{2,1,0:T(8,128)}, f32[1,32]{1,0:T(1,128)}, f32[32,32,81]{2,1,0:T(8,12...) custom-call(f32[16,2,1024]{2,1,0:T(2,128)} %get-tuple-element.27.refs_0_, ...), custom_call_target="tpu_custom_call" | custom-call | tf_op jit(solution)/shard_map/deliver/pallas_call | solution.py:734
